TPU v7x, 128 devices: a whole 4x4x4 slice. The times are simulated.
128 devices in a mesh: ctx: 32 (over y, z_hi, x), tp: 4 (over z_lo, core).
Axes of the slice: x: 4, y: 4, z: 4 (z_hi: 2, z_lo: 2; z = z_hi * 2 + z_lo), core: 2. Of those that a mesh axis runs over, the one named last changes fastest.
Arguments:
- query_rot: bfloat16 [16384, 3072], P('ctx', 'tp'), may hold values from -12 to 12
- key_rot: bfloat16 [16384, 3072], P('ctx', 'tp'), may hold values from -12 to 12
- value: bfloat16 [16384, 3072], P('ctx', 'tp'), may hold values from -6 to 6
- grad_out: bfloat16 [16384, 3072], P('ctx', 'tp'), may hold values from -6 to 6
- text_key: bfloat16 [256, 3072], P('ctx', 'tp'), may hold values from -6 to 6
- text_value: bfloat16 [256, 3072], P('ctx', 'tp'), may hold values from -6 to 6
- positions: int32 [3, 16384], P(None, 'ctx'), may hold values from 0 to 63, as said below
- tile_mask: int32 [128, 128], replicated, may hold values from 0 to 1, as said below
Outputs:
- grad_query: bfloat16 [16384, 3072], P('ctx', 'tp')
- grad_key: bfloat16 [16384, 3072], P('ctx', 'tp')
- grad_value: bfloat16 [16384, 3072], P('ctx', 'tp')
- grad_text_key: bfloat16 [256, 3072], P('ctx', 'tp')
- grad_text_value: bfloat16 [256, 3072], P('ctx', 'tp')
Inputs may be any that keep to these rules, and one draw needn't show every extreme that they name: tile_mask[a, b] is 1 when tiles a and b lie in the same frame (2 tiles a frame, in token order) and 0 when their frames are more than 2 apart. positions[0, n] is n // 256; positions[1, n] and positions[2, n] are the row and column of token n in its frame of rows of 16 tokens, each plus an offset of 0 to 31 common to all tokens.
All inputs are finite; a program needn't handle non-finite values.
Results may differ from a plain program's by a relative error of at most 0.02.
Values may be sent and summed in bfloat16 or wider, within the bound.
No kernel may reach another device: no remote copies, remote signals or barrier semaphores. Data moves between devices by JAX's collectives and lax.ppermute only.
A program may use at most 128 MiB of HBM per device.

v0:
```python
import jax
import jax.numpy as jnp
from jax import lax
from jax.sharding import PartitionSpec as P

D_HEAD = 128
TILE = 128
ROPE_THETA = 256.0
TIME_STRETCH = 0.25


def shifted(block, axis, distance):
    devices = range(lax.axis_size(axis))
    route = [(i - distance, i) for i in devices if i - distance in devices]
    return lax.ppermute(block, axis, route)


def rope_tables(positions, head_dim):
    time_dims = head_dim // 8
    plane_dims = (head_dim - time_dims) // 2
    layout = ((time_dims, TIME_STRETCH), (plane_dims, 1.0), (plane_dims, 1.0))
    angle_parts = []
    for axis_id in range(3):
        seg_width, stretch = layout[axis_id]
        pair_ids = jnp.arange(seg_width // 2, dtype=jnp.float32)
        frequency = ROPE_THETA ** (-2.0 * pair_ids / seg_width)
        scaled_pos = positions[axis_id].astype(jnp.float32) * stretch
        angle_parts.append(scaled_pos[:, None] * frequency[None, :])
    angles = jnp.concatenate(angle_parts, axis=1)
    return (jnp.cos(angles), jnp.sin(angles))


def unrotate(grad_rot, cosine, sine):
    tok_rows = grad_rot.shape[0]
    pairs = grad_rot.reshape(tok_rows, -1, cosine.shape[1], 2)
    even_part = pairs[..., 0]
    odd_part = pairs[..., 1]
    cos_rows = cosine[:, None, :]
    sin_rows = sine[:, None, :]
    turned = jnp.stack(
        [cos_rows * even_part + sin_rows * odd_part, cos_rows * odd_part - sin_rows * even_part],
        axis=-1,
    )
    return turned.reshape(grad_rot.shape)


def scores_of(query_head, key_head):
    return jnp.einsum(
        "qd,kd->qk", query_head, key_head, preferred_element_type=jnp.float32
    ) * D_HEAD ** (-0.5)


def piece_grads(query_head, grad_head, weights, row_delta, key_head, value_head):
    score_scale = D_HEAD ** (-0.5)
    dprobs = jnp.einsum("qd,kd->qk", grad_head, value_head, preferred_element_type=jnp.float32)
    dscores = (weights.astype(jnp.float32) * (dprobs - row_delta[:, None])).astype(jnp.bfloat16)
    results = []
    results.append(jnp.dot(dscores, key_head, preferred_element_type=jnp.float32) * score_scale)
    results.append(
        jnp.einsum("qk,qd->kd", dscores, query_head, preferred_element_type=jnp.float32)
        * score_scale
    )
    results.append(jnp.einsum("qk,qd->kd", weights, grad_head, preferred_element_type=jnp.float32))
    return tuple(results)


def shards(query_rot, key_rot, value, grad_out, text_key, text_value, positions, tile_mask):
    tok_rows = query_rot.shape[0]
    head_count = query_rot.shape[1] // D_HEAD
    tile_rows = tok_rows // TILE
    ctx_index = lax.axis_index("ctx")
    text_keys, text_values = (
        lax.all_gather(text_key, "ctx", axis=0, tiled=True),
        lax.all_gather(text_value, "ctx", axis=0, tiled=True),
    )
    left_keys, left_values = shifted((key_rot, value), "ctx", 1)
    right_keys, right_values = shifted((key_rot, value), "ctx", -1)
    padded_mask = jnp.pad(tile_mask, ((tile_rows, tile_rows), (tile_rows, tile_rows)))

    def window(col_shift):
        mask_block = lax.dynamic_slice(
            padded_mask,
            ((ctx_index + 1) * tile_rows, (ctx_index + col_shift + 1) * tile_rows),
            (tile_rows, tile_rows),
        )
        return jnp.repeat(jnp.repeat(mask_block, TILE, axis=0), TILE, axis=1) > 0

    allow_left = window(-1)
    allow_own = window(0)
    allow_right = window(1)
    query_parts, own_key_parts, own_value_parts = ([], [], [])
    left_key_parts, left_value_parts, right_key_parts, right_value_parts = ([], [], [], [])
    text_key_parts, text_value_parts, total_parts, delta_parts = ([], [], [], [])
    for head_id in range(head_count):
        head_cols = slice(head_id * D_HEAD, (head_id + 1) * D_HEAD)
        query_head = query_rot[:, head_cols]
        grad_head = grad_out[:, head_cols]
        text_key_head = text_keys[:, head_cols]
        text_value_head = text_values[:, head_cols]
        sides = (
            (left_keys[:, head_cols], left_values[:, head_cols], allow_left),
            (key_rot[:, head_cols], value[:, head_cols], allow_own),
            (right_keys[:, head_cols], right_values[:, head_cols], allow_right),
        )
        masked = []
        for key_head, value_head, allowed in sides:
            masked.append(jnp.where(allowed, scores_of(query_head, key_head), -jnp.inf))
        text_scores = scores_of(query_head, text_key_head)
        row_max = jnp.max(text_scores, axis=1)
        for piece_scores in masked:
            row_max = jnp.maximum(row_max, jnp.max(piece_scores, axis=1))
        row_total = jnp.sum(jnp.exp(text_scores - row_max[:, None]), axis=1)
        for piece_scores in masked:
            row_total = row_total + jnp.sum(jnp.exp(piece_scores - row_max[:, None]), axis=1)
        log_total = row_max + jnp.log(row_total)
        weight_list = [
            jnp.exp(piece_scores - log_total[:, None]).astype(jnp.bfloat16)
            for piece_scores in masked
        ]
        text_weights = jnp.exp(text_scores - log_total[:, None]).astype(jnp.bfloat16)
        attended = jnp.dot(text_weights, text_value_head, preferred_element_type=jnp.float32)
        for slot in range(3):
            attended = attended + jnp.dot(
                weight_list[slot], sides[slot][1], preferred_element_type=jnp.float32
            )
        row_delta = jnp.sum(grad_head.astype(jnp.float32) * attended, axis=1)
        total_parts.append(log_total)
        delta_parts.append(row_delta)
        text_terms = piece_grads(
            query_head, grad_head, text_weights, row_delta, text_key_head, text_value_head
        )
        query_grad = text_terms[0]
        text_key_parts.append(text_terms[1])
        text_value_parts.append(text_terms[2])
        for slot in range(3):
            key_head, value_head, allowed = sides[slot]
            terms = piece_grads(
                query_head, grad_head, weight_list[slot], row_delta, key_head, value_head
            )
            query_grad = query_grad + terms[0]
            if slot == 0:
                left_key_parts.append(terms[1])
                left_value_parts.append(terms[2])
            if slot == 1:
                own_key_parts.append(terms[1])
                own_value_parts.append(terms[2])
            if slot == 2:
                right_key_parts.append(terms[1])
                right_value_parts.append(terms[2])
        query_parts.append(query_grad)
    query_grad_all = jnp.concatenate(query_parts, axis=1)
    key_grad_all = jnp.concatenate(own_key_parts, axis=1)
    value_grad_all = jnp.concatenate(own_value_parts, axis=1)
    right_back = (
        shifted(jnp.concatenate(left_key_parts, axis=1).astype(jnp.bfloat16), "ctx", -1).astype(
            jnp.float32
        ),
        shifted(jnp.concatenate(left_value_parts, axis=1).astype(jnp.bfloat16), "ctx", -1).astype(
            jnp.float32
        ),
    )
    left_back = (
        shifted(jnp.concatenate(right_key_parts, axis=1).astype(jnp.bfloat16), "ctx", 1).astype(
            jnp.float32
        ),
        shifted(jnp.concatenate(right_value_parts, axis=1).astype(jnp.bfloat16), "ctx", 1).astype(
            jnp.float32
        ),
    )
    key_grad_all = key_grad_all + right_back[0] + left_back[0]
    value_grad_all = value_grad_all + right_back[1] + left_back[1]
    text_key_grad, text_value_grad = (
        lax.psum_scatter(
            jnp.concatenate(text_key_parts, axis=1).astype(jnp.bfloat16),
            "ctx",
            scatter_dimension=0,
            tiled=True,
        ).astype(jnp.float32),
        lax.psum_scatter(
            jnp.concatenate(text_value_parts, axis=1).astype(jnp.bfloat16),
            "ctx",
            scatter_dimension=0,
            tiled=True,
        ).astype(jnp.float32),
    )
    cosine, sine = rope_tables(positions, D_HEAD)
    grad_query = unrotate(query_grad_all, cosine, sine).astype(jnp.bfloat16)
    grad_key = unrotate(key_grad_all, cosine, sine).astype(jnp.bfloat16)
    return (
        grad_query,
        grad_key,
        value_grad_all.astype(jnp.bfloat16),
        text_key_grad.astype(jnp.bfloat16),
        text_value_grad.astype(jnp.bfloat16),
    )


def solution(mesh):
    placed = (
        P("ctx", "tp"),
        P("ctx", "tp"),
        P("ctx", "tp"),
        P("ctx", "tp"),
        P("ctx", "tp"),
        P("ctx", "tp"),
        P(None, "ctx"),
        P(),
    )
    return jax.shard_map(
        shards,
        mesh=mesh,
        in_specs=placed,
        out_specs=(P("ctx", "tp"), P("ctx", "tp"), P("ctx", "tp"), P("ctx", "tp"), P("ctx", "tp")),
        check_vma=False,
    )
```

profile of v0, /device:TPU:0, one launch (start us, length us, event | category | flops | bytes accessed | tf_op | source)
XLA Modules:
  0.0 775.8 jit_solution(6786113106563927850)
XLA Ops:
  8.7 5.5 collective-permute-start
  14.2 3.5 collective-permute-start.2
  18.9 118.4 %all_gather.6 = bf16[256,768]{1,0:T(8,128)(2,1)S(1)} all-gather(bf16[8,768]{1,0:T(8,128)(2,1)} %param.12), channel_id=1, replica_groups=mesh['ctx'=32,'tp'=4] {'ctx'}, dimensions={0}, use_global_device_ids=true | all-gather | bytes 405504 | tf_op jit(solution)/shard_map/all_gather | solution.py:73
  137.3 1.9 fusion.352
  144.5 94.3 %all_gather.7 = bf16[256,768]{1,0:T(8,128)(2,1)} all-gather(bf16[8,768]{1,0:T(8,128)(2,1)S(1)} %copy-done.75), channel_id=1, replica_groups=mesh['ctx'=32,'tp'=4] {'ctx'}, dimensions={0}, use_global_device_ids=true | all-gather | bytes 405504 | tf_op jit(solution)/shard_map/all_gather | solution.py:74
  241.1 1.9 fusion.351
  243.0 1.9 fusion.347
  244.9 1.8 fusion.343
  246.7 1.9 fusion.355
  250.3 2.2 fusion.363
  325.4 1.9 copy.153
  328.6 1.9 fusion.130
  345.4 5.8 collective-permute-start.7
  395.6 2.2 reshape.347
  397.8 5.7 collective-permute-start.5
  403.6 2.2 fusion.50
  405.8 2.1 fusion.49
  408.9 1.8 add_convert_fusion
  412.5 3.3 convert_add_fusion
  415.8 2.3 reshape.348
  418.1 4.3 add_convert_fusion.1
  422.4 3.6 pad_maximum_fusion
  429.0 116.1 %reduce-scatter.9.cloned.1.call-done = bf16[8,768]{1,0:T(8,128)(2,1)} async-done(((bf16[256,768]{1,0:T(8,128)(2,1)}), bf16[8,768]{1,0:T(8,128)(2,1)}) %reduce-scatter.9.cloned.1.call-update) | async-done | bytes 12304
  545.0 223.7 %reduce-scatter.7.cloned.1.call-done = bf16[8,768]{1,0:T(8,128)(2,1)} async-done(((bf16[256,768]{1,0:T(8,128)(2,1)}), bf16[8,768]{1,0:T(8,128)(2,1)}) %reduce-scatter.7.cloned.1.call-update) | async-done | bytes 12304
  (389 shorter events, 149.5 us)
Async XLA Ops:
  7.2 133.8 %copy-start.1 = (bf16[512,768]{1,0:T(8,128)(2,1)S(1)}, bf16[512,768]{1,0:T(8,128)(2,1)}, u32[]{:S(2)}) copy-start(bf16[512,768]{1,0:T(8,128)(2,1)} %param.8) | copy-start | bytes 2359300
  7.2 135.5 %copy-start.85 = (s32[3,512]{1,0:T(4,128)S(1)}, s32[3,512]{1,0:T(4,128)}, u32[]{:S(2)}) copy-start(s32[3,512]{1,0:T(4,128)} %param.14) | copy-start | bytes 18436
  7.2 135.5 %copy-start.69 = (s32[128,128]{1,0:T(8,128)S(1)}, s32[128,128]{1,0:T(8,128)}, u32[]{:S(2)}) copy-start(s32[128,128]{1,0:T(8,128)} %param.15) | copy-start | bytes 196612
  7.2 137.3 %copy-start.75 = (bf16[8,768]{1,0:T(8,128)(2,1)S(1)}, bf16[8,768]{1,0:T(8,128)(2,1)}, u32[]{:S(2)}) copy-start(bf16[8,768]{1,0:T(8,128)(2,1)} %param.13) | copy-start | bytes 36868
  7.2 231.6 %copy-start = (bf16[512,768]{1,0:T(8,128)(2,1)S(1)}, bf16[512,768]{1,0:T(8,128)(2,1)}, u32[]{:S(2)}) copy-start(bf16[512,768]{1,0:T(8,128)(2,1)} %param.11) | copy-start | bytes 2359300
  7.2 537.8 %reduce-scatter.9.cloned.1.call-start = ((), (), s32[]{:S(2)}) async-start(), calls=%async_computation.3 | async-start | bytes 405504
  7.3 256.0 %collective-permute-start.1 = (bf16[512,768]{1,0:T(8,128)(2,1)}, bf16[512,768]{1,0:T(8,128)(2,1)}, u32[]{:S(2)}, u32[]{:S(2)}) collective-permute-start(bf16[512,768]{1,0:T(8,128)(2,1)} %param.9), channel_id=1, source_target_pairs={{4,0},{8,4},{12,8},{16,12},{20,16},{24,20},{28,24},{32,28},{36,32}... | collective-permute-start | bytes 2359304 | tf_op jit(solution)/shard_map/ppermute | solution.py:15
  8.7 255.9 %collective-permute-start = (bf16[512,768]{1,0:T(8,128)(2,1)}, bf16[512,768]{1,0:T(8,128)(2,1)}, u32[]{:S(2)}, u32[]{:S(2)}) collective-permute-start(bf16[512,768]{1,0:T(8,128)(2,1)} %param.9), channel_id=1, source_target_pairs={{0,4},{4,8},{8,12},{12,16},{16,20},{20,24},{24,28},{28,32},{32,36}... | collective-permute-start | bytes 2359304 | tf_op jit(solution)/shard_map/ppermute | solution.py:15
  14.2 272.3 %collective-permute-start.2 = (bf16[512,768]{1,0:T(8,128)(2,1)}, bf16[512,768]{1,0:T(8,128)(2,1)}, u32[]{:S(2)}, u32[]{:S(2)}) collective-permute-start(bf16[512,768]{1,0:T(8,128)(2,1)} %param.10), channel_id=1, source_target_pairs={{0,4},{4,8},{8,12},{12,16},{16,20},{20,24},{24,28},{28,32},{32,36}... | collective-permute-start | bytes 2359304 | tf_op jit(solution)/shard_map/ppermute | solution.py:15
  17.6 272.4 %collective-permute-start.3 = (bf16[512,768]{1,0:T(8,128)(2,1)}, bf16[512,768]{1,0:T(8,128)(2,1)}, u32[]{:S(2)}, u32[]{:S(2)}) collective-permute-start(bf16[512,768]{1,0:T(8,128)(2,1)} %param.10), channel_id=1, source_target_pairs={{4,0},{8,4},{12,8},{16,12},{20,16},{24,20},{28,24},{32,28},{36,32}... | collective-permute-start | bytes 2359304 | tf_op jit(solution)/shard_map/ppermute | solution.py:15
  141.0 100.1 %copy-start.50 = (bf16[512,768]{1,0:T(8,128)(2,1)S(1)}, bf16[512,768]{1,0:T(8,128)(2,1)}, u32[]{:S(2)}) copy-start(bf16[512,768]{1,0:T(8,128)(2,1)} %param.9) | copy-start | bytes 2359300
  267.0 40.5 %copy-start.9 = (bf16[512,512]{0,1:T(8,128)(2,1)}, bf16[512,512]{0,1:T(8,128)(2,1)S(1)}, u32[]{:S(2)}) copy-start(bf16[512,512]{0,1:T(8,128)(2,1)S(1)} %get-tuple-element.71) | copy-start | bytes 1572868
  267.1 44.2 %copy-start.11 = (bf16[512,512]{0,1:T(8,128)(2,1)}, bf16[512,512]{0,1:T(8,128)(2,1)S(1)}, u32[]{:S(2)}) copy-start(bf16[512,512]{0,1:T(8,128)(2,1)S(1)} %get-tuple-element.70) | copy-start | bytes 1572868
  271.1 43.2 %copy-start.13 = (bf16[512,512]{0,1:T(8,128)(2,1)}, bf16[512,512]{0,1:T(8,128)(2,1)S(1)}, u32[]{:S(2)}) copy-start(bf16[512,512]{0,1:T(8,128)(2,1)S(1)} %get-tuple-element.74) | copy-start | bytes 1572868
  271.1 45.7 %copy-start.7 = (bf16[512,512]{0,1:T(8,128)(2,1)}, bf16[512,512]{0,1:T(8,128)(2,1)S(1)}, u32[]{:S(2)}) copy-start(bf16[512,512]{0,1:T(8,128)(2,1)S(1)} %get-tuple-element.72) | copy-start | bytes 1572868
  285.5 17.8 %copy-start.25 = (bf16[512,512]{0,1:T(8,128)(2,1)}, bf16[512,512]{0,1:T(8,128)(2,1)S(1)}, u32[]{:S(2)}) copy-start(bf16[512,512]{0,1:T(8,128)(2,1)S(1)} %get-tuple-element.68) | copy-start | bytes 1572868
  285.5 19.3 %copy-start.17 = (bf16[512,512]{0,1:T(8,128)(2,1)}, bf16[512,512]{0,1:T(8,128)(2,1)S(1)}, u32[]{:S(2)}) copy-start(bf16[512,512]{0,1:T(8,128)(2,1)S(1)} %get-tuple-element.66) | copy-start | bytes 1572868
  285.5 20.7 %copy-start.33 = (bf16[512,512]{0,1:T(8,128)(2,1)}, bf16[512,512]{0,1:T(8,128)(2,1)S(1)}, u32[]{:S(2)}) copy-start(bf16[512,512]{0,1:T(8,128)(2,1)S(1)} %get-tuple-element.67) | copy-start | bytes 1572868
  289.5 12.4 %copy-start.35 = (bf16[512,512]{0,1:T(8,128)(2,1)}, bf16[512,512]{0,1:T(8,128)(2,1)S(1)}, u32[]{:S(2)}) copy-start(bf16[512,512]{0,1:T(8,128)(2,1)S(1)} %get-tuple-element.64) | copy-start | bytes 1572868
  327.3 441.4 %reduce-scatter.7.cloned.1.call-start = ((), (), s32[]{:S(2)}) async-start(), calls=%async_computation.2 | async-start | bytes 405504
  337.5 71.4 %collective-permute-start.6 = (bf16[512,768]{0,1:T(8,128)(2,1)}, bf16[512,768]{0,1:T(8,128)(2,1)}, u32[]{:S(2)}, u32[]{:S(2)}) collective-permute-start(bf16[512,768]{0,1:T(8,128)(2,1)} %fusion.102), channel_id=1, source_target_pairs={{4,0},{8,4},{12,8},{16,12},{20,16},{24,20},{28,24},{32,28},{36,32}... | collective-permute-start | bytes 2359304 | tf_op jit(solution)/shard_map/ppermute | solution.py:15
  345.4 63.6 %collective-permute-start.7 = (bf16[512,768]{0,1:T(8,128)(2,1)}, bf16[512,768]{0,1:T(8,128)(2,1)}, u32[]{:S(2)}, u32[]{:S(2)}) collective-permute-start(bf16[512,768]{0,1:T(8,128)(2,1)} %fusion.96), channel_id=1, source_target_pairs={{0,4},{4,8},{8,12},{12,16},{16,20},{20,24},{24,28},{28,32},{32,36}... | collective-permute-start | bytes 2359304 | tf_op jit(solution)/shard_map/ppermute | solution.py:15
  366.7 45.2 %collective-permute-start.4 = (bf16[512,768]{0,1:T(8,128)(2,1)}, bf16[512,768]{0,1:T(8,128)(2,1)}, u32[]{:S(2)}, u32[]{:S(2)}) collective-permute-start(bf16[512,768]{0,1:T(8,128)(2,1)} %fusion.83), channel_id=1, source_target_pairs={{4,0},{8,4},{12,8},{16,12},{20,16},{24,20},{28,24},{32,28},{36,32}... | collective-permute-start | bytes 2359304 | tf_op jit(solution)/shard_map/ppermute | solution.py:15
  397.8 14.7 %collective-permute-start.5 = (bf16[512,768]{0,1:T(8,128)(2,1)}, bf16[512,768]{0,1:T(8,128)(2,1)}, u32[]{:S(2)}, u32[]{:S(2)}) collective-permute-start(bf16[512,768]{0,1:T(8,128)(2,1)} %copy-done.74), channel_id=1, source_target_pairs={{0,4},{4,8},{8,12},{12,16},{16,20},{20,24},{24,28},{28,32},{32,36}... | collective-permute-start | bytes 2359304 | tf_op jit(solution)/shard_map/ppermute | solution.py:15
  (72 other events, 281.3 us)
Sparse Core Ops, SparseCore 0:
  327.4 217.5 reduce-scatter.8
  551.1 217.5 reduce-scatter.6
where the time goes:
time: 787 us; the launch traced here: 776 us
  waiting for transfers between devices  340 us (43%)
  blocking collectives  213 us (27%)
  matrix products  132 us (17%)
  local copies, waits for them, and re-layouts  26.5 us (3%)
  starting transfers between devices  25.8 us (3%)
  other arithmetic  21.7 us (3%)
  between operations  16.1 us (2%)
    unnamed x4, waiting for transfers between devices  340 us
    all_gather x1, blocking collectives, shards(): lax.all_gather(text_key, 'ctx', axis=0, tiled=True)  118 us
    all_gather x1, blocking collectives, shards(): lax.all_gather(text_value, 'ctx', axis=0, tiled=True)  94.3 us
    dot_general x24, matrix products, scores_of(): jnp.einsum('qd,kd->qk', query_head, key_head, preferred_element_type=jnp....  32.9 us
    ppermute x8, starting transfers between devices, shifted(): return lax.ppermute(block, axis, route)  25.7 us
    dot_general x24, matrix products, piece_grads(): jnp.einsum('qd,kd->qk', grad_head, value_head, preferred_element_type=jnp...  24.8 us
    unnamed x190, local copies, waits for them, and re-layouts  21.1 us
    dot_general x24, matrix products, piece_grads(): jnp.einsum('qk,qd->kd', weights, grad_head, preferred_element_type=jnp.fl...  19.3 us
  transfers between devices with their start and end apart: 10, of which 3 were waited for; matrix products, arithmetic and copies ran while one was open for 18% of the time, Pallas kernels for 0%

commit v1 on v0

--- a/solution.py
+++ b/solution.py
@@ -70,7 +70,9 @@
     tile_rows = tok_rows // TILE
     ctx_index = lax.axis_index("ctx")
     text_keys, text_values = (
-        lax.all_gather(text_key, "ctx", axis=0, tiled=True),
+        jnp.concatenate(
+            lax.all_to_all(jnp.stack([text_key] * lax.axis_size("ctx")), "ctx", 0, 0), axis=0
+        ),
         lax.all_gather(text_value, "ctx", axis=0, tiled=True),
     )
     left_keys, left_values = shifted((key_rot, value), "ctx", 1)

time: 787 us -> 681 us (0.87)
  blocking collectives: 213 us -> 102 us
  starting transfers between devices: 25.8 us -> 41 us
    all_gather x1 -> x0, blocking collectives: 118 us -> none  [shards(): lax.all_gather(text_key, 'ctx', axis=0, tiled=True)]
    all_to_all x0 -> x1, starting transfers between devices: none -> 15.2 us  [shards(): lax.all_to_all(jnp.stack([text_key] * lax.axis_size('ctx')), 'ctx', 0, 0)]
    all_gather x1, blocking collectives: 94.3 us -> 102 us  [shards(): lax.all_gather(text_value, 'ctx', axis=0, tiled=True)]
    unnamed x190 -> x184, local copies, waits for them, and re-layouts: 21.1 us -> 16.9 us
  transfers between devices with their start and end apart: 10 -> 11, of which waited for: 3 -> 3; matrix products, arithmetic and copies ran while one was open for 18% -> 21% of each run, Pallas kernels for 0% -> 0%
where the time goes in v1:
time: 681 us; the launch traced here: 675 us
  waiting for transfers between devices  337 us (49%)
  matrix products  130 us (19%)
  blocking collectives  102 us (15%)
  starting transfers between devices  41 us (6%)
  other arithmetic  25.6 us (4%)
  local copies, waits for them, and re-layouts  23.8 us (3%)
  between operations  16.1 us (2%)
    unnamed x4, waiting for transfers between devices  336 us
    all_gather x1, blocking collectives, shards(): lax.all_gather(text_value, 'ctx', axis=0, tiled=True)  102 us
    dot_general x24, matrix products, scores_of(): jnp.einsum('qd,kd->qk', query_head, key_head, preferred_element_type=jnp....  27.8 us
    ppermute x8, starting transfers between devices, shifted(): return lax.ppermute(block, axis, route)  25.7 us
    dot_general x24, matrix products, piece_grads(): jnp.einsum('qd,kd->qk', grad_head, value_head, preferred_element_type=jnp...  25.4 us
    dot_general x24, matrix products, piece_grads(): jnp.dot(dscores, key_head, preferred_element_type=jnp.float32) * score_scale  20.2 us
    dot_general x24, matrix products, piece_grads(): jnp.einsum('qk,qd->kd', weights, grad_head, preferred_element_type=jnp.fl...  19.2 us
    dot_general x24, matrix products, piece_grads(): jnp.einsum('qk,qd->kd', dscores, query_head, preferred_element_type=jnp.f...  18.8 us
  transfers between devices with their start and end apart: 11, of which 3 were waited for; matrix products, arithmetic and copies ran while one was open for 21% of the time, Pallas kernels for 0%

profile of v1, /device:TPU:0, one launch (start us, length us, event | category | flops | bytes accessed | tf_op | source)
XLA Modules:
  0.0 675.5 jit_solution(3524048408977127849)
XLA Ops:
  8.6 5.5 collective-permute-start
  14.1 3.5 collective-permute-start.2
  20.3 15.2 %all-to-all-start = ((bf16[32,8,768]{2,1,0:T(8,128)(2,1)}), bf16[32,8,768]{2,1,0:T(8,128)(2,1)S(1)}, u32[]{:S(2)}, u32[]{:S(2)}) async-start(bf16[32,8,768]{2,1,0:T(8,128)(2,1)} %stack.8), calls=%async_computation | async-start | bytes 786432 | tf_op jit(solution)/shard_map/all_to_all | solution.py:74
  41.5 1.9 fusion.351
  43.3 1.8 fusion.347
  45.2 1.9 fusion.343
  47.0 1.9 fusion.355
  50.2 2.2 fusion.363
  58.9 2.0 fusion.205
  60.9 102.3 %all_gather.3 = bf16[256,768]{1,0:T(8,128)(2,1)} all-gather(bf16[8,768]{1,0:T(8,128)(2,1)} %param.13), channel_id=1, replica_groups=mesh['ctx'=32,'tp'=4] {'ctx'}, dimensions={0}, use_global_device_ids=true | all-gather | bytes 405504 | tf_op jit(solution)/shard_map/all_gather | solution.py:76
  227.5 1.9 copy.153
  230.8 1.9 fusion.130
  248.5 5.6 collective-permute-start.7
  298.6 2.2 reshape.353
  300.8 5.8 collective-permute-start.5
  306.7 2.2 fusion.50
  308.8 2.1 fusion.49
  312.0 1.8 add_convert_fusion
  315.5 3.3 convert_add_fusion
  318.9 2.3 reshape.354
  321.2 4.3 add_convert_fusion.1
  325.4 3.6 pad_maximum_fusion
  332.0 112.7 %reduce-scatter.9.cloned.1.call-done = bf16[8,768]{1,0:T(8,128)(2,1)} async-done(((bf16[256,768]{1,0:T(8,128)(2,1)}), bf16[8,768]{1,0:T(8,128)(2,1)}) %reduce-scatter.9.cloned.1.call-update) | async-done | bytes 12304
  444.7 223.7 %reduce-scatter.7.cloned.1.call-done = bf16[8,768]{1,0:T(8,128)(2,1)} async-done(((bf16[256,768]{1,0:T(8,128)(2,1)}), bf16[8,768]{1,0:T(8,128)(2,1)}) %reduce-scatter.7.cloned.1.call-update) | async-done | bytes 12304
  (385 shorter events, 148.0 us)
Async XLA Ops:
  7.2 31.9 %copy-start = (bf16[512,768]{1,0:T(8,128)(2,1)S(1)}, bf16[512,768]{1,0:T(8,128)(2,1)}, u32[]{:S(2)}) copy-start(bf16[512,768]{1,0:T(8,128)(2,1)} %param.11) | copy-start | bytes 2359300
  7.2 34.3 %copy-start.48 = (bf16[512,768]{1,0:T(8,128)(2,1)S(1)}, bf16[512,768]{1,0:T(8,128)(2,1)}, u32[]{:S(2)}) copy-start(bf16[512,768]{1,0:T(8,128)(2,1)} %param.9) | copy-start | bytes 2359300
  7.2 34.3 %copy-start.1 = (bf16[512,768]{1,0:T(8,128)(2,1)S(1)}, bf16[512,768]{1,0:T(8,128)(2,1)}, u32[]{:S(2)}) copy-start(bf16[512,768]{1,0:T(8,128)(2,1)} %param.8) | copy-start | bytes 2359300
  7.2 157.5 %collective-permute-start.1 = (bf16[512,768]{1,0:T(8,128)(2,1)}, bf16[512,768]{1,0:T(8,128)(2,1)}, u32[]{:S(2)}, u32[]{:S(2)}) collective-permute-start(bf16[512,768]{1,0:T(8,128)(2,1)} %param.9), channel_id=1, source_target_pairs={{4,0},{8,4},{12,8},{16,12},{20,16},{24,20},{28,24},{32,28},{36,32}... | collective-permute-start | bytes 2359304 | tf_op jit(solution)/shard_map/ppermute | solution.py:15
  8.6 157.4 %collective-permute-start = (bf16[512,768]{1,0:T(8,128)(2,1)}, bf16[512,768]{1,0:T(8,128)(2,1)}, u32[]{:S(2)}, u32[]{:S(2)}) collective-permute-start(bf16[512,768]{1,0:T(8,128)(2,1)} %param.9), channel_id=1, source_target_pairs={{0,4},{4,8},{8,12},{12,16},{16,20},{20,24},{24,28},{28,32},{32,36}... | collective-permute-start | bytes 2359304 | tf_op jit(solution)/shard_map/ppermute | solution.py:15
  14.1 173.2 %collective-permute-start.2 = (bf16[512,768]{1,0:T(8,128)(2,1)}, bf16[512,768]{1,0:T(8,128)(2,1)}, u32[]{:S(2)}, u32[]{:S(2)}) collective-permute-start(bf16[512,768]{1,0:T(8,128)(2,1)} %param.10), channel_id=1, source_target_pairs={{0,4},{4,8},{8,12},{12,16},{16,20},{20,24},{24,28},{28,32},{32,36}... | collective-permute-start | bytes 2359304 | tf_op jit(solution)/shard_map/ppermute | solution.py:15
  17.6 173.5 %collective-permute-start.3 = (bf16[512,768]{1,0:T(8,128)(2,1)}, bf16[512,768]{1,0:T(8,128)(2,1)}, u32[]{:S(2)}, u32[]{:S(2)}) collective-permute-start(bf16[512,768]{1,0:T(8,128)(2,1)} %param.10), channel_id=1, source_target_pairs={{4,0},{8,4},{12,8},{16,12},{20,16},{24,20},{28,24},{32,28},{36,32}... | collective-permute-start | bytes 2359304 | tf_op jit(solution)/shard_map/ppermute | solution.py:15
  20.3 142.9 %all-to-all-start = ((bf16[32,8,768]{2,1,0:T(8,128)(2,1)}), bf16[32,8,768]{2,1,0:T(8,128)(2,1)S(1)}, u32[]{:S(2)}, u32[]{:S(2)}) async-start(bf16[32,8,768]{2,1,0:T(8,128)(2,1)} %stack.8), calls=%async_computation | async-start | bytes 786432 | tf_op jit(solution)/shard_map/all_to_all | solution.py:74
  35.5 409.1 %reduce-scatter.9.cloned.1.call-start = ((), (), s32[]{:S(2)}) async-start(), calls=%async_computation.4 | async-start | bytes 405504
  168.4 41.3 %copy-start.9 = (bf16[512,512]{0,1:T(8,128)(2,1)}, bf16[512,512]{0,1:T(8,128)(2,1)S(1)}, u32[]{:S(2)}) copy-start(bf16[512,512]{0,1:T(8,128)(2,1)S(1)} %get-tuple-element.71) | copy-start | bytes 1572868
  168.4 45.0 %copy-start.11 = (bf16[512,512]{0,1:T(8,128)(2,1)}, bf16[512,512]{0,1:T(8,128)(2,1)S(1)}, u32[]{:S(2)}) copy-start(bf16[512,512]{0,1:T(8,128)(2,1)S(1)} %get-tuple-element.70) | copy-start | bytes 1572868
  172.4 44.1 %copy-start.13 = (bf16[512,512]{0,1:T(8,128)(2,1)}, bf16[512,512]{0,1:T(8,128)(2,1)S(1)}, u32[]{:S(2)}) copy-start(bf16[512,512]{0,1:T(8,128)(2,1)S(1)} %get-tuple-element.74) | copy-start | bytes 1572868
  172.4 46.6 %copy-start.7 = (bf16[512,512]{0,1:T(8,128)(2,1)}, bf16[512,512]{0,1:T(8,128)(2,1)S(1)}, u32[]{:S(2)}) copy-start(bf16[512,512]{0,1:T(8,128)(2,1)S(1)} %get-tuple-element.72) | copy-start | bytes 1572868
  186.7 18.1 %copy-start.25 = (bf16[512,512]{0,1:T(8,128)(2,1)}, bf16[512,512]{0,1:T(8,128)(2,1)S(1)}, u32[]{:S(2)}) copy-start(bf16[512,512]{0,1:T(8,128)(2,1)S(1)} %get-tuple-element.68) | copy-start | bytes 1572868
  186.7 19.5 %copy-start.17 = (bf16[512,512]{0,1:T(8,128)(2,1)}, bf16[512,512]{0,1:T(8,128)(2,1)S(1)}, u32[]{:S(2)}) copy-start(bf16[512,512]{0,1:T(8,128)(2,1)S(1)} %get-tuple-element.66) | copy-start | bytes 1572868
  186.7 21.7 %copy-start.33 = (bf16[512,512]{0,1:T(8,128)(2,1)}, bf16[512,512]{0,1:T(8,128)(2,1)S(1)}, u32[]{:S(2)}) copy-start(bf16[512,512]{0,1:T(8,128)(2,1)S(1)} %get-tuple-element.67) | copy-start | bytes 1572868
  190.6 10.7 %copy-start.19 = (bf16[512,512]{0,1:T(8,128)(2,1)}, bf16[512,512]{0,1:T(8,128)(2,1)S(1)}, u32[]{:S(2)}) copy-start(bf16[512,512]{0,1:T(8,128)(2,1)S(1)} %get-tuple-element.63) | copy-start | bytes 1572868
  190.6 12.9 %copy-start.35 = (bf16[512,512]{0,1:T(8,128)(2,1)}, bf16[512,512]{0,1:T(8,128)(2,1)S(1)}, u32[]{:S(2)}) copy-start(bf16[512,512]{0,1:T(8,128)(2,1)S(1)} %get-tuple-element.64) | copy-start | bytes 1572868
  194.1 83.6 %copy-start.39 = (bf16[512,512]{0,1:T(8,128)(2,1)}, bf16[512,512]{0,1:T(8,128)(2,1)S(1)}, u32[]{:S(2)}) copy-start(bf16[512,512]{0,1:T(8,128)(2,1)S(1)} %fusion.19) | copy-start | bytes 1572868
  229.5 438.9 %reduce-scatter.7.cloned.1.call-start = ((), (), s32[]{:S(2)}) async-start(), calls=%async_computation.3 | async-start | bytes 405504
  240.7 71.3 %collective-permute-start.6 = (bf16[512,768]{0,1:T(8,128)(2,1)}, bf16[512,768]{0,1:T(8,128)(2,1)}, u32[]{:S(2)}, u32[]{:S(2)}) collective-permute-start(bf16[512,768]{0,1:T(8,128)(2,1)} %fusion.102), channel_id=1, source_target_pairs={{4,0},{8,4},{12,8},{16,12},{20,16},{24,20},{28,24},{32,28},{36,32}... | collective-permute-start | bytes 2359304 | tf_op jit(solution)/shard_map/ppermute | solution.py:15
  248.5 63.4 %collective-permute-start.7 = (bf16[512,768]{0,1:T(8,128)(2,1)}, bf16[512,768]{0,1:T(8,128)(2,1)}, u32[]{:S(2)}, u32[]{:S(2)}) collective-permute-start(bf16[512,768]{0,1:T(8,128)(2,1)} %fusion.96), channel_id=1, source_target_pairs={{0,4},{4,8},{8,12},{12,16},{16,20},{20,24},{24,28},{28,32},{32,36}... | collective-permute-start | bytes 2359304 | tf_op jit(solution)/shard_map/ppermute | solution.py:15
  269.6 45.3 %collective-permute-start.4 = (bf16[512,768]{0,1:T(8,128)(2,1)}, bf16[512,768]{0,1:T(8,128)(2,1)}, u32[]{:S(2)}, u32[]{:S(2)}) collective-permute-start(bf16[512,768]{0,1:T(8,128)(2,1)} %fusion.83), channel_id=1, source_target_pairs={{4,0},{8,4},{12,8},{16,12},{20,16},{24,20},{28,24},{32,28},{36,32}... | collective-permute-start | bytes 2359304 | tf_op jit(solution)/shard_map/ppermute | solution.py:15
  300.8 14.7 %collective-permute-start.5 = (bf16[512,768]{0,1:T(8,128)(2,1)}, bf16[512,768]{0,1:T(8,128)(2,1)}, u32[]{:S(2)}, u32[]{:S(2)}) collective-permute-start(bf16[512,768]{0,1:T(8,128)(2,1)} %copy-done.77), channel_id=1, source_target_pairs={{0,4},{4,8},{8,12},{12,16},{16,20},{20,24},{24,28},{28,32},{32,36}... | collective-permute-start | bytes 2359304 | tf_op jit(solution)/shard_map/ppermute | solution.py:15
  (70 other events, 289.3 us)
Sparse Core Ops, SparseCore 0:
  229.6 215.0 reduce-scatter.8
  450.7 217.6 reduce-scatter.6
